TPU v7x, 128 devices: a whole 4x4x4 slice. The times are simulated.
128 devices in a mesh: loader: 16 (over z, x), shard: 8 (over y, core).
Axes of the slice: x: 4, y: 4, z: 4, core: 2. Of those that a mesh axis runs over, the one named last changes fastest.
Arguments:
- hidden_states: bfloat16 [262144, 768], P(('loader', 'shard')), may hold values from -6 to 6
- w_in: bfloat16 [768, 3072], replicated, may hold values from -0.21875 to 0.21875
- w_out: bfloat16 [3072, 768], replicated, may hold values from -0.109375 to 0.109375
- ln_gain: float32 [768], replicated, may hold values from 0.1 to 1.9
- passage_rows: int32 [1024], P(('loader', 'shard')), may hold values from 0 to 32767, as said below
- old_index: bfloat16 [32768, 768], P('shard'), may hold values from -1.2 to 1.2
- queries: bfloat16 [4096, 768], P('loader'), may hold values from -256 to 256
- candidates: int32 [4096, 64], P('loader'), may hold values from 0 to 32767, as said below
- teacher: float32 [4096, 64], P('loader'), may hold values from -8 to 304
Outputs:
- new_index: bfloat16 [32768, 768], P('shard')
- distill_loss: float32 [4096], P(('loader', 'shard'))
- query_grad: float32 [4096, 768], P(('loader', 'shard'))
Inputs may be any that keep to these rules, and one draw needn't show every extreme that they name: `passage_rows`: distinct rows of the index; row r belongs to shard r // 4096. The 8 passages of one device name at most 2 rows of any one shard, and exactly 2 of some shard. `candidates`: rows of the index; a query may name a row twice.
All inputs are finite; a program needn't handle non-finite values.
Results may differ from a plain program's by a relative error of at most 0.0075.
Values may be sent and summed in bfloat16 or wider, within the bound.
A program may use at most 192 MiB of HBM per device.

v0:
```python
import jax
import jax.numpy as jnp
from jax import lax
from jax.sharding import PartitionSpec as P

LEN = 256


epsilon = 1e-05


def encode_block(token_rows, w_in, w_out, ln_gain):
    inner_rows = jax.nn.gelu(
        jnp.dot(token_rows, w_in, preferred_element_type=jnp.float32), approximate=False
    ).astype(jnp.bfloat16)
    mixed_rows = token_rows.astype(jnp.float32) + jnp.dot(
        inner_rows, w_out, preferred_element_type=jnp.float32
    )
    centered = mixed_rows - jnp.mean(mixed_rows, axis=-1, keepdims=True)
    spread = jnp.mean(centered * centered, axis=-1, keepdims=True)
    normed = centered * lax.rsqrt(spread + epsilon) * ln_gain
    model_width = normed.shape[-1]
    return jnp.mean(normed.reshape(-1, LEN, model_width), axis=1).astype(jnp.bfloat16)


def distill(scores, teacher):
    log_student = jax.nn.log_softmax(scores, axis=-1)
    log_teacher = jax.nn.log_softmax(teacher, axis=-1)
    weight_teacher = jnp.exp(log_teacher)
    loss_rows = jnp.sum(weight_teacher * (log_teacher - log_student), axis=-1)
    weight_diff = (jnp.exp(log_student) - weight_teacher).astype(jnp.bfloat16)
    return (loss_rows, weight_diff)


def weigh_rows(weight_diff, masked_rows):
    return jnp.einsum("qk,qkd->qd", weight_diff, masked_rows, preferred_element_type=jnp.float32)


def local(
    hidden_states, w_in, w_out, ln_gain, passage_rows, old_index, queries, candidates, teacher
):
    fresh_rows = encode_block(hidden_states, w_in, w_out, ln_gain)
    shard_rows = old_index.shape[0]
    shard_count = lax.axis_size("shard")
    my_shard = lax.axis_index("shard")
    base_row = my_shard * shard_rows
    all_fresh, all_ids = (
        lax.all_gather(fresh_rows, ("loader", "shard"), axis=0, tiled=True),
        lax.all_gather(passage_rows, ("loader", "shard"), axis=0, tiled=True),
    )
    local_rows = all_ids - base_row
    keep_rows = (all_ids >= 0) & (local_rows >= 0) & (local_rows < shard_rows)
    local_rows = jnp.where(keep_rows, local_rows, shard_rows)
    new_index = old_index.at[local_rows].set(all_fresh, mode="drop")
    cand_local = candidates - base_row
    mine_mask = (cand_local >= 0) & (cand_local < shard_rows)
    picked = jnp.take(new_index, jnp.where(mine_mask, cand_local, 0), axis=0)
    masked_rows = jnp.where(mine_mask[:, :, None], picked, jnp.zeros((), jnp.bfloat16))
    per_device = queries.shape[0] // shard_count
    first_row = my_shard * per_device
    partial_scores = jnp.einsum(
        "qd,qkd->qk", queries, masked_rows, preferred_element_type=jnp.float32
    )
    scores = lax.psum(partial_scores, "shard")
    loss_all, weight_diff = distill(scores, teacher)
    distill_loss = lax.dynamic_slice_in_dim(loss_all, first_row, per_device, 0)
    query_grad = lax.psum_scatter(
        weigh_rows(weight_diff, masked_rows), "shard", scatter_dimension=0, tiled=True
    )
    return (new_index, distill_loss, query_grad)


def solution(mesh):
    return jax.shard_map(
        local,
        mesh=mesh,
        in_specs=(
            P(("loader", "shard"), None),
            P(),
            P(),
            P(),
            P(("loader", "shard")),
            P("shard", None),
            P("loader", None),
            P("loader", None),
            P("loader", None),
        ),
        out_specs=(P("shard", None), P(("loader", "shard")), P(("loader", "shard"), None)),
        check_vma=False,
    )
```

profile of v0, /device:TPU:1, one launch (start us, length us, event | category | flops | bytes accessed | tf_op | source)
XLA Modules:
  0.0 383.7 jit_solution(12507223585201137285)
XLA Ops:
  7.2 5.9 %copy.30 = bf16[4096,768]{1,0:T(8,128)(2,1)} copy(bf16[4096,768]{1,0:T(8,128)(2,1)} %param.15) | data formatting | bytes 12582912
  13.2 62.7 %fusion.21.clone.4 = bf16[2048,3072]{1,0:T(8,128)(2,1)} fusion(bf16[2048,768]{1,0:T(8,128)(2,1)} %param.10, bf16[768,3072]{1,0:T(8,128)(2,1)} %param.11), kind=kOutput, calls=%fused_computation.5.clone.clone.clone.clone.clone.clone.1 | convolution fusion | flops 10072621056 | bytes 20447232 | tf_op jit(solution)/shard_map/dot_general | solution.py:14
  76.0 13.3 %fusion.58 = (f32[2048]{0:T(1024)S(1)}, f32[2048,768]{1,0:T(8,128)S(1)}) fusion(bf16[3072,768]{1,0:T(8,128)(2,1)S(1)} %copy-done.4, bf16[2048,768]{1,0:T(8,128)(2,1)S(1)} %copy-done.5, bf16[2048,3072]{1,0:T(8,128)(2,1)} %fusion.21.clone.4), kind=kOutput, calls=%fused_computation.84 | convolution fusion | flops 9668392960 | bytes 26746880 | tf_op jit(solution)/shard_map/dot_general | solution.py:16
  89.3 0.8 multiply_reduce_fusion
  90.1 1.2 bitcast_reduce_fusion
  91.4 0.6 multiply_convert_fusion
  92.3 0.1 copy.14
  92.4 0.1 copy.15
  92.6 0.2 dynamic-update-slice
  92.9 69.4 %all-reduce = s32[1024]{0:T(1024)S(1)} all-reduce(s32[1024]{0:T(1024)S(1)} %dynamic-update-slice), channel_id=1, replica_groups=mesh['loader'=16,'shard'=8] {'loader','shard'}, use_global_device_ids=true, to_apply=%add | all-reduce | flops 1024 | bytes 8192
  162.4 12.4 %scatter_fusion = bf16[4096,768]{1,0:T(8,128)(2,1)} fusion(bf16[4096,768]{1,0:T(8,128)(2,1)} %copy.30, s32[1024]{0:T(1024)S(1)} %compare_select_fusion.1, bf16[1024,768]{1,0:T(8,128)(2,1)} %all-gather.2.cloned.1.call-done), kind=kCustom, calls=%fused_computation.1 | custom fusion | bytes 4722688 | tf_op jit(solution)/shard_map/scatter | solution.py:54
  174.8 76.7 %gather_fusion = bf16[16384,768]{1,0:T(8,128)(2,1)} fusion(bf16[4096,768]{1,0:T(8,128)(2,1)} %scatter_fusion, s32[16384]{0:T(1024)S(1)} %broadcast_clamp_fusion), kind=kCustom, calls=%fused_computation | custom fusion | bytes 50397184 | tf_op jit(solution)/shard_map/jit(_take)/gather | solution.py:57
  251.5 17.4 %select_select_fusion.5 = bf16[256,64,768]{2,1,0:T(8,128)(2,1)} fusion(bf16[256,64,768]{2,1,0:T(8,128)(2,1)} %bitcast.24, pred[256,64]{1,0:T(8,128)(4,1)S(1)} %copy.15, pred[256,64]{1,0:T(8,128)(4,1)S(1)} %copy.14), kind=kLoop, calls=%fused_computation.6.clone.1.clone.1 | loop fusion | flops 25165824 | bytes 50364416 | tf_op jit(solution)/shard_map/qd,qkd->qk/dot_general | solution.py:61
  268.9 11.7 %fusion.11 = f32[256,1,64]{2,1,0:T(1,128)S(1)} fusion(bf16[256,768,1]{1,0,2:T(8,128)(2,1)S(1)} %bitcast.23, bf16[256,64,768]{2,1,0:T(8,128)(2,1)} %select_select_fusion.5), kind=kOutput, calls=%fused_computation.23 | convolution fusion | flops 25165824 | bytes 25624576 | tf_op jit(solution)/shard_map/qd,qkd->qk/dot_general | solution.py:61
  280.6 0.7 copy.18
  281.4 52.7 %all-reduce.3.cloned.1.call-done = f32[256,64]{0,1:T(8,128)} async-done(((f32[256,64]{0,1:T(8,128)}), f32[256,64]{0,1:T(8,128)}) %all-reduce.3.cloned.1.call-update) | async-done | bytes 65552 | tf_op jit(solution)/shard_map/psum | solution.py:64
  334.1 0.9 reduce_max.14
  335.0 0.9 exponential_reduce_fusion
  335.9 0.9 fusion.23
  336.8 0.1 copy.19
  336.9 9.4 %fusion.10 = f32[256,1,768]{2,1,0:T(1,128)S(1)} fusion(bf16[256,64,1]{1,2,0:T(2,128)(2,1)S(1)} %copy.19, bf16[256,64,768]{2,1,0:T(8,128)(2,1)} %bitcast.25, pred[256,64]{1,0:T(8,128)(4,1)S(1)} %copy.15, pred[256,64]{1,0:T(8,128)(4,1)S(1)} %copy.14), kind=kOutput, calls=%fused_computation.22 | convolution fusion | flops 50331648 | bytes 26017792 | tf_op jit(solution)/shard_map/qk,qkd->qd/dot_general | solution.py:36
  346.3 0.9 copy.25
  347.3 0.6 dynamic_slice.3
  347.9 29.3 %reduce-scatter.2.cloned.1.call-done = f32[32,768]{1,0:T(8,128)} async-done(((f32[256,768]{1,0:T(8,128)}), f32[32,768]{1,0:T(8,128)}) %reduce-scatter.2.cloned.1.call-update) | async-done | bytes 98320 | tf_op jit(solution)/shard_map/reduce_scatter | solution.py:67
  (33 shorter events, 0.6 us)
Async XLA Ops:
  7.2 261.7 %copy-start = (bf16[256,768]{1,0:T(8,128)(2,1)S(1)}, bf16[256,768]{1,0:T(8,128)(2,1)}, u32[]{:S(2)}) copy-start(bf16[256,768]{1,0:T(8,128)(2,1)} %param.16) | copy-start | bytes 1179652
  7.2 155.2 %all-gather.2.cloned.1.call-start = ((), (), s32[]{:S(2)}) async-start(), calls=%async_computation.1 | async-start | bytes 1585152 | tf_op jit(solution)/shard_map/all_gather | solution.py:48
  13.2 62.8 %copy-start.4 = (bf16[3072,768]{1,0:T(8,128)(2,1)S(1)}, bf16[3072,768]{1,0:T(8,128)(2,1)}, u32[]{:S(2)}) copy-start(bf16[3072,768]{1,0:T(8,128)(2,1)} %param.12) | copy-start | bytes 14155780
  13.2 62.8 %copy-start.5 = (bf16[2048,768]{1,0:T(8,128)(2,1)S(1)}, bf16[2048,768]{1,0:T(8,128)(2,1)}, u32[]{:S(2)}) copy-start(bf16[2048,768]{1,0:T(8,128)(2,1)} %param.10) | copy-start | bytes 9437188
  75.9 14.2 %copy-start.3 = (f32[768]{0:T(1024)S(1)}, f32[768]{0:T(1024)}, u32[]{:S(2)}) copy-start(f32[768]{0:T(1024)} %param.13) | copy-start | bytes 9220
  75.9 16.1 %copy-start.2 = (s32[256,64]{0,1:T(8,128)S(1)}, s32[256,64]{0,1:T(8,128)}, u32[]{:S(2)}) copy-start(s32[256,64]{0,1:T(8,128)} %param.17) | copy-start | bytes 196612
  75.9 16.6 %copy-start.1 = (f32[256,64]{0,1:T(8,128)S(1)}, f32[256,64]{0,1:T(8,128)}, u32[]{:S(2)}) copy-start(f32[256,64]{0,1:T(8,128)} %param.18) | copy-start | bytes 196612
  75.9 16.7 %copy-start.6 = (s32[8]{0:T(128)S(1)}, s32[8]{0:T(128)}, u32[]{:S(2)}) copy-start(s32[8]{0:T(128)} %param.14) | copy-start | bytes 100
  92.0 242.1 %all-reduce.3.cloned.1.call-start = ((), (), s32[]{:S(2)}) async-start(), calls=%async_computation.2 | async-start | bytes 131072 | tf_op jit(solution)/shard_map/psum | solution.py:64
  281.3 95.8 %reduce-scatter.2.cloned.1.call-start = ((), (), s32[]{:S(2)}) async-start(), calls=%async_computation.3 | async-start | bytes 884736 | tf_op jit(solution)/shard_map/reduce_scatter | solution.py:67
Sparse Core Ops, SparseCore 0:
  92.1 67.8 all-gather.1
  281.5 52.6 all-reduce.2
  347.4 29.7 reduce-scatter.1
where the time goes:
time: 386 us; the launch traced here: 384 us
  local copies, waits for them, and re-layouts  98.1 us (25%)
  matrix products  97.2 us (25%)
  waiting for transfers between devices  82.1 us (21%)
  blocking collectives  69.4 us (18%)
  other arithmetic  22.8 us (6%)
  between operations  13.9 us (4%)
    gather x1, local copies, waits for them, and re-layouts, local(): picked = jnp.take(new_index, jnp.where(mine_mask, cand_local, 0), axis=0)  76.7 us
    unnamed x1, blocking collectives  69.4 us
    dot_general x1, matrix products, encode_block(): jnp.dot(token_rows, w_in, preferred_element_type=jnp.float32)  62.7 us
    psum x1, waiting for transfers between devices, local(): scores = lax.psum(partial_scores, 'shard')  52.7 us
    reduce_scatter x1, waiting for transfers between devices, local(): lax.psum_scatter(weigh_rows(weight_diff, masked_rows), 'shard', scatter_d...  29.3 us
    dot_general x1, other arithmetic, local(): jnp.einsum('qd,qkd->qk', queries, masked_rows, preferred_element_type=jnp...  17.4 us
    dot_general x1, matrix products, encode_block(): jnp.dot(inner_rows, w_out, preferred_element_type=jnp.float32)  13.3 us
    scatter x1, local copies, waits for them, and re-layouts, local(): new_index = old_index.at[local_rows].set(all_fresh, mode='drop')  12.4 us
  transfers between devices with their start and end apart: 3, of which 2 were waited for; matrix products, arithmetic and copies ran while one was open for 0% of the time, Pallas kernels for 0%

commit v1 on v0

v1 whole, which is shorter than its diff:
```python
import functools

import jax
import jax.numpy as jnp
from jax import lax
from jax.experimental import pallas as pl
from jax.experimental.pallas import tpu as pltpu
from jax.sharding import PartitionSpec as P

LEN = 256
EPS = 1e-05
MIB = 2**20
MESH = pl.DeviceIdType.MESH
BF16, F32, I32 = jnp.bfloat16, jnp.float32, jnp.int32
TAIL = 128
FLAG = 8192
NONE = -1e30


def gelu(v):
    return 0.5 * v * (1.0 + lax.erf(v * 0.7071067811865476))


def encode_kernel(block, chunk, shards, shard_rows, x_hbm, win_hbm, wout_hbm, gain_ref, rows_ref,
                  out_ref, x, win, wout, inner, mixed, fresh, slots, sem):
    tokens, d = x.shape
    ff = win.shape[1]
    blocks, chunks = tokens // block, ff // chunk
    jobs = [pltpu.make_async_copy(x_hbm, x, sem.at[0]),
            pltpu.make_async_copy(win_hbm, win, sem.at[1]),
            pltpu.make_async_copy(wout_hbm, wout, sem.at[2])]
    for job in jobs:
        job.start()
    for job in jobs:
        job.wait()

    def norm(b):
        for j in range(block // LEN):
            y = mixed[b % 2, j * LEN:(j + 1) * LEN, :]
            centered = y - jnp.mean(y, axis=-1, keepdims=True)
            spread = jnp.mean(centered * centered, axis=-1, keepdims=True)
            normed = centered * lax.rsqrt(spread + EPS)
            k = b * (block // LEN) + j
            fresh[k:k + 1, :] = jnp.sum(normed, axis=0, keepdims=True) * (1.0 / LEN) * gain_ref[...]

    for b in range(blocks):
        rows = slice(b * block, (b + 1) * block)
        for c in range(chunks):
            cols = slice(c * chunk, (c + 1) * chunk)
            h = jnp.dot(x[rows, :], win[:, cols], preferred_element_type=F32)
            inner[b % 2, :, cols] = gelu(h).astype(BF16)
            if c == 0 and b > 0:
                norm(b - 1)
        mixed[b % 2] = x[rows, :].astype(F32) + jnp.dot(
            inner[b % 2], wout[...], preferred_element_type=F32)
    norm(blocks - 1)

    passages = tokens // LEN
    ids = [rows_ref[p] for p in range(passages)]
    owner = [i // shard_rows for i in ids]
    lane = lax.broadcasted_iota(I32, (1, TAIL), 1)
    slot_iota = lax.broadcasted_iota(I32, (2 * shards, d + TAIL), 0)
    filled = jnp.zeros((2 * shards, d + TAIL), F32)
    for p in range(passages):
        rank = sum([(owner[q] == owner[p]).astype(I32) for q in range(p)], jnp.int32(0))
        place = owner[p] * 2 + rank
        local = ids[p] - owner[p] * shard_rows
        tail = jnp.where(lane == 0, local // 64, jnp.where(lane == 1, local % 64, jnp.where(lane == 2, 1, 0)))
        row = jnp.concatenate([fresh[p:p + 1, :], tail.astype(F32)], axis=1)
        filled = jnp.where(slot_iota == place, row, filled)
    slots[...] = filled.astype(BF16).astype(F32)
    for s in range(shards):
        out_ref[s] = slots[2 * s:2 * s + 2, :]


def encode(shards, shard_rows, hidden, w_in, w_out, gain, passage_rows):
    tokens, d = hidden.shape
    ff = w_in.shape[1]
    block, chunk = 512, 768
    anywhere = pl.BlockSpec(memory_space=pl.ANY)
    return pl.pallas_call(
        functools.partial(encode_kernel, block, chunk, shards, shard_rows),
        out_shape=jax.ShapeDtypeStruct((shards, 2, d + TAIL), F32),
        in_specs=[anywhere] * 3 + [pl.BlockSpec(memory_space=pltpu.VMEM), pl.BlockSpec(memory_space=pltpu.SMEM)],
        out_specs=pl.BlockSpec(memory_space=pltpu.VMEM),
        scratch_shapes=[
            pltpu.VMEM((tokens, d), BF16),
            pltpu.VMEM((d, ff), BF16),
            pltpu.VMEM((ff, d), BF16),
            pltpu.VMEM((2, block, ff), BF16),
            pltpu.VMEM((2, block, d), F32),
            pltpu.VMEM((tokens // LEN, d), F32),
            pltpu.VMEM((2 * shards, d + TAIL), F32),
            pltpu.SemaphoreType.DMA((3,)),
        ],
        compiler_params=pltpu.CompilerParams(vmem_limit_bytes=56 * MIB),
        name="encode",
    )(hidden, w_in, w_out, gain.reshape(1, d), passage_rows)


def exchange_kernel(loaders, shards, slots_ref, out_ref, mine, packed, send1, recv1, send2, recv2):
    li, si = lax.axis_index("loader"), lax.axis_index("shard")
    barrier = pltpu.get_barrier_semaphore()
    for k in range(1, shards):
        pl.semaphore_signal(barrier, inc=1, device_id=(li, lax.rem(si + k, shards)), device_id_type=MESH)
    for k in range(1, loaders):
        pl.semaphore_signal(barrier, inc=1, device_id=(lax.rem(li + k, loaders), si), device_id_type=MESH)
    pl.semaphore_wait(barrier, shards + loaders - 2)
    first = []
    for k in range(1, shards):
        to = lax.rem(si + k, shards)
        copy = pltpu.make_async_remote_copy(
            src_ref=slots_ref.at[to], dst_ref=mine.at[si], send_sem=send1.at[k], recv_sem=recv1.at[k],
            device_id=(li, to), device_id_type=MESH)
        copy.start()
        first.append(copy)
    mine[si] = slots_ref[si]
    for copy in first:
        copy.wait_recv()
    for s in range(shards):
        packed[2 * s:2 * s + 2, :] = mine[s]
    out_ref[li] = packed[...].astype(BF16)
    second = []
    for k in range(1, loaders):
        copy = pltpu.make_async_remote_copy(
            src_ref=out_ref.at[li], dst_ref=out_ref.at[li], send_sem=send2.at[k], recv_sem=recv2.at[k],
            device_id=(lax.rem(li + k, loaders), si), device_id_type=MESH)
        copy.start()
        second.append(copy)
    for copy in second:
        copy.wait_recv()
    for copy in first + second:
        copy.wait_send()


def exchange(loaders, shards, slots):
    width = slots.shape[-1]
    return pl.pallas_call(
        functools.partial(exchange_kernel, loaders, shards),
        out_shape=jax.ShapeDtypeStruct((loaders, 2 * shards, width), BF16),
        in_specs=[pl.BlockSpec(memory_space=pltpu.VMEM)],
        out_specs=pl.BlockSpec(memory_space=pltpu.VMEM),
        scratch_shapes=[
            pltpu.VMEM((shards, 2, width), F32),
            pltpu.VMEM((2 * shards, width), F32),
            pltpu.SemaphoreType.DMA((shards,)),
            pltpu.SemaphoreType.DMA((shards,)),
            pltpu.SemaphoreType.DMA((loaders,)),
            pltpu.SemaphoreType.DMA((loaders,)),
        ],
        compiler_params=pltpu.CompilerParams(collective_id=0, has_side_effects=True),
        name="exchange",
    )(slots)


def both_halves(x):
    return jnp.concatenate([x, x], axis=1)


def score_kernel(tile, fresh_ref, q_ref, cand_ref, teacher_ref, old_hbm,
                 new_hbm, score_ref, stats_ref, old, new, s_all, hi_s, lo_s, got, in_sem, out_sem):
    rows, d = old.shape
    nq = q_ref.shape[0]
    k = cand_ref.shape[0]
    tiles = rows // tile
    loads = [pltpu.make_async_copy(old_hbm.at[pl.ds(t * tile, tile)], old.at[pl.ds(t * tile, tile)], in_sem.at[t])
             for t in range(tiles)]
    for load in loads:
        load.start()
    base = lax.axis_index("shard") * rows
    local = cand_ref[...] - base
    local_q = jnp.concatenate([local, local], axis=0).T
    hi_s[...] = local_q >> 7
    lo_s[...] = local_q & 127

    lane = lax.broadcasted_iota(I32, (8, TAIL), 1)
    digits = jnp.where(lane == 0, 64.0, jnp.where(lane == 1, 1.0, jnp.where(lane == 2, float(FLAG), 0.0))).astype(BF16)
    where_to = lax.dot_general(digits, fresh_ref[:, d:d + TAIL], (((1,), (1,)), ((), ())),
                               preferred_element_type=F32)[0:1, :].astype(I32)
    slots = fresh_ref.shape[0]
    ones = jnp.ones((slots, 128), BF16)
    row_iota = lax.broadcasted_iota(I32, (tile, slots), 0)
    stores = []
    for t in range(tiles):
        rs = slice(t * tile, (t + 1) * tile)
        place = jnp.where(row_iota + (t * tile + FLAG) == where_to, 1.0, 0.0).astype(BF16)
        put = jnp.dot(place, fresh_ref[:, 0:d], preferred_element_type=F32)
        has = jnp.dot(place, ones, preferred_element_type=F32)
        loads[t].wait()
        for c in range(d // 128):
            cs = slice(c * 128, (c + 1) * 128)
            new[rs, cs] = jnp.where(has > 0.5, put[:, cs], old[rs, cs].astype(F32)).astype(BF16)
        store = pltpu.make_async_copy(new.at[pl.ds(t * tile, tile)], new_hbm.at[pl.ds(t * tile, tile)], out_sem.at[t])
        store.start()
        stores.append(store)
        s_all[:, rs] = lax.dot_general(q_ref[...], new[rs, :], (((1,), (1,)), ((), ())), preferred_element_type=F32)

    def pick(g, carry):
        qs = pl.ds(pl.multiple_of(g * 8, 8), 8)
        hi, lo = hi_s[qs, :], lo_s[qs, :]
        out = jnp.zeros((8, 128), F32)
        for h in range(rows // 128):
            got_h = jnp.take_along_axis(s_all[qs, h * 128:(h + 1) * 128], lo, axis=1, mode="promise_in_bounds")
            out = jnp.where(hi == h, got_h, out)
        got[qs, :] = out
        return carry

    lax.fori_loop(0, nq // 8, pick, 0)
    score = got[...].T[0:k, :]
    owned = (local >= 0) & (local < rows)
    score_ref[...] = score
    teacher = teacher_ref[...]
    shifted = teacher - jnp.max(teacher, axis=0, keepdims=True)
    log_t = shifted - jnp.log(jnp.sum(jnp.exp(shifted), axis=0, keepdims=True))
    p_t = jnp.exp(log_t)
    top = jnp.max(jnp.where(owned, score, NONE), axis=0, keepdims=True)
    diff = score - top
    z = jnp.sum(jnp.where(owned, jnp.exp(jnp.where(owned, diff, 0.0)), 0.0), axis=0, keepdims=True)
    a = jnp.sum(jnp.where(owned, p_t * diff, 0.0), axis=0, keepdims=True)
    b = jnp.sum(jnp.where(owned, p_t, 0.0), axis=0, keepdims=True)
    e = jnp.sum(p_t * log_t, axis=0, keepdims=True)
    stats_ref[...] = jnp.concatenate([top, z, a, b, e, e, e, e], axis=0)
    for store in stores:
        store.wait()


def score(fresh, queries, cand_t, teacher_t, old_index):
    rows, d = old_index.shape
    nq = queries.shape[0]
    k = cand_t.shape[0]
    tile = 512
    anywhere = pl.BlockSpec(memory_space=pl.ANY)
    vmem = pl.BlockSpec(memory_space=pltpu.VMEM)
    return pl.pallas_call(
        functools.partial(score_kernel, tile),
        out_shape=[
            jax.ShapeDtypeStruct((rows, d), BF16),
            jax.ShapeDtypeStruct((k, nq), F32),
            jax.ShapeDtypeStruct((8, nq), F32),
        ],
        in_specs=[vmem] * 4 + [anywhere],
        out_specs=[anywhere, vmem, vmem],
        scratch_shapes=[
            pltpu.VMEM((rows, d), BF16),
            pltpu.VMEM((rows, d), BF16),
            pltpu.VMEM((nq, rows), F32),
            pltpu.VMEM((nq, 2 * k), I32),
            pltpu.VMEM((nq, 2 * k), I32),
            pltpu.VMEM((nq, 2 * k), F32),
            pltpu.SemaphoreType.DMA((rows // tile,)),
            pltpu.SemaphoreType.DMA((rows // tile,)),
        ],
        compiler_params=pltpu.CompilerParams(vmem_limit_bytes=56 * MIB),
        name="score",
    )(fresh, queries, cand_t, teacher_t, old_index)


def grad_kernel(shards, score_ref, stats_ref, cand_ref, teacher_ref, new_hbm, loss_ref, grad_ref,
                new, stats, w_s, hi_s, lo_s, spread, part, own, inbox,
                load_sem, send1, recv1, send2, recv2):
    rows, d = new.shape
    k, nq = score_ref.shape
    per = nq // shards
    li, si = lax.axis_index("loader"), lax.axis_index("shard")
    load = pltpu.make_async_copy(new_hbm, new, load_sem)
    load.start()
    barrier = pltpu.get_barrier_semaphore()
    for j in range(1, shards):
        pl.semaphore_signal(barrier, inc=1, device_id=(li, lax.rem(si + j, shards)), device_id_type=MESH)
    pl.semaphore_wait(barrier, shards - 1)
    first = []
    for j in range(1, shards):
        copy = pltpu.make_async_remote_copy(
            src_ref=stats_ref, dst_ref=stats.at[si], send_sem=send1.at[j], recv_sem=recv1.at[j],
            device_id=(li, lax.rem(si + j, shards)), device_id_type=MESH)
        copy.start()
        first.append(copy)
    stats[si] = stats_ref[...]

    local = cand_ref[...] - si * rows
    owned = (local >= 0) & (local < rows)
    local_q = jnp.concatenate([local, local], axis=0).T
    hi_s[...] = local_q >> 7
    lo_s[...] = (local_q & 127).astype(F32)
    teacher = teacher_ref[...]
    shifted = teacher - jnp.max(teacher, axis=0, keepdims=True)
    p_t = jnp.exp(shifted - jnp.log(jnp.sum(jnp.exp(shifted), axis=0, keepdims=True)))
    for copy in first:
        copy.wait_recv()
    every = [stats[s] for s in range(shards)]
    top = functools.reduce(jnp.maximum, [e[0:1] for e in every])
    z = sum([e[1:2] * jnp.exp(e[0:1] - top) for e in every])
    cross = sum([e[2:3] + e[3:4] * (e[0:1] - top) for e in every])
    log_z = jnp.log(z)
    loss = stats_ref[4:5, :] - cross + log_z
    out = jnp.zeros((1, per), F32)
    for s in range(shards):
        out = jnp.where(si == s, loss[:, s * per:(s + 1) * per], out)
    loss_ref[...] = out
    student = jnp.exp(jnp.where(owned, score_ref[...] - top - log_z, 0.0))
    weight = jnp.where(owned, student - p_t, 0.0).astype(BF16).astype(F32)
    w_s[...] = jnp.concatenate([weight, weight], axis=0).T

    lane = lax.broadcasted_iota(I32, (8, 2 * k), 1)
    sub = lax.broadcasted_iota(I32, (8, 2 * k), 0)
    masks = [lane // k + 2 * v == sub for v in range(4)]
    lo_iota = lax.broadcasted_iota(I32, (128, 8 * k), 0).astype(F32)
    his = rows // 128

    def group(q0):
        qs = pl.ds(pl.multiple_of(q0, 8), 8)
        w2, hi2, lo2 = w_s[qs, :], hi_s[qs, :], lo_s[qs, :]
        wide = jnp.concatenate([jnp.where(m, w2, 0.0) for m in masks], axis=1)
        low = jnp.concatenate(
            [jnp.sum(jnp.where(m, lo2, 0.0), axis=0, keepdims=True) for m in masks], axis=1)
        hi_wide = jnp.concatenate([hi2] * 4, axis=1)
        left = jnp.concatenate([jnp.where(hi_wide == h, wide, 0.0) for h in range(his)], axis=0).astype(BF16)
        right = jnp.where(lo_iota == low, 1.0, 0.0).astype(BF16)
        return lax.dot_general(left, right, (((1,), (1,)), ((), ())), preferred_element_type=F32)

    def place(g, carry):
        one, two = group(g * 16), group(g * 16 + 8)
        qs = pl.ds(pl.multiple_of(g * 16, 16), 16)
        for h in range(his):
            both = jnp.concatenate([one[h * 8:(h + 1) * 8], two[h * 8:(h + 1) * 8]], axis=0)
            spread[qs, h * 128:(h + 1) * 128] = both.astype(BF16)
        return carry

    lax.fori_loop(0, nq // 16, place, 0)
    load.wait()
    total = jnp.dot(spread[...], new[...], preferred_element_type=F32)
    mine = jnp.zeros((per, d), F32)
    for s in range(shards):
        block = total[s * per:(s + 1) * per, :]
        part[s] = block.astype(BF16)
        mine = jnp.where(si == s, block, mine)
    own[...] = mine
    second = []
    for j in range(1, shards):
        to = lax.rem(si + j, shards)
        copy = pltpu.make_async_remote_copy(
            src_ref=part.at[to], dst_ref=inbox.at[j], send_sem=send2.at[j], recv_sem=recv2.at[j],
            device_id=(li, to), device_id_type=MESH)
        copy.start()
        second.append(copy)
    got = own[...]
    for j, copy in enumerate(second):
        copy.wait_recv()
        got = got + inbox[j + 1].astype(F32)
    grad_ref[...] = got
    for copy in first + second:
        copy.wait_send()


def gradient(shards, scores, stats, cand_t, teacher_t, new_index):
    rows, d = new_index.shape
    k, nq = scores.shape
    per = nq // shards
    vmem = pl.BlockSpec(memory_space=pltpu.VMEM)
    return pl.pallas_call(
        functools.partial(grad_kernel, shards),
        out_shape=[jax.ShapeDtypeStruct((1, per), F32), jax.ShapeDtypeStruct((per, d), F32)],
        in_specs=[vmem] * 4 + [pl.BlockSpec(memory_space=pl.ANY)],
        out_specs=[vmem, vmem],
        scratch_shapes=[
            pltpu.VMEM((rows, d), BF16),
            pltpu.VMEM((shards, 8, nq), F32),
            pltpu.VMEM((nq, 2 * k), F32),
            pltpu.VMEM((nq, 2 * k), I32),
            pltpu.VMEM((nq, 2 * k), F32),
            pltpu.VMEM((nq, rows), BF16),
            pltpu.VMEM((shards, per, d), BF16),
            pltpu.VMEM((per, d), F32),
            pltpu.VMEM((shards, per, d), BF16),
            pltpu.SemaphoreType.DMA,
            pltpu.SemaphoreType.DMA((shards,)),
            pltpu.SemaphoreType.DMA((shards,)),
            pltpu.SemaphoreType.DMA((shards,)),
            pltpu.SemaphoreType.DMA((shards,)),
        ],
        compiler_params=pltpu.CompilerParams(collective_id=1, has_side_effects=True, vmem_limit_bytes=56 * MIB),
        name="gradient",
    )(scores, stats, cand_t, teacher_t, new_index)


def solution(mesh):
    loaders, shards = mesh.shape["loader"], mesh.shape["shard"]

    def local(hidden_states, w_in, w_out, ln_gain, passage_rows, old_index, queries, candidates, teacher):
        cand_t, teacher_t = candidates.T, teacher.T
        slots = encode(shards, old_index.shape[0], hidden_states, w_in, w_out, ln_gain, passage_rows)
        fresh = exchange(loaders, shards, slots)
        fresh = fresh.reshape(loaders * 2 * shards, fresh.shape[-1])
        new_index, scores, stats = score(fresh, queries, cand_t, teacher_t, old_index)
        loss, grad = gradient(shards, scores, stats, cand_t, teacher_t, new_index)
        return new_index, loss.reshape(-1), grad

    return jax.shard_map(
        local,
        mesh=mesh,
        in_specs=(
            P(("loader", "shard"), None),
            P(),
            P(),
            P(),
            P(("loader", "shard")),
            P("shard", None),
            P("loader", None),
            P("loader", None),
            P("loader", None),
        ),
        out_specs=(P("shard", None), P(("loader", "shard")), P(("loader", "shard"), None)),
        check_vma=False,
    )
```

time: 386 us -> 87.1 us (0.23)
  matrix products: 97.2 us -> 0 us
  local copies, waits for them, and re-layouts: 98.1 us -> 3.91 us
  Pallas kernels: 0 us -> 82.2 us
  waiting for transfers between devices: 82.1 us -> 0 us
  blocking collectives: 69.4 us -> 0 us
  other arithmetic: 22.8 us -> 0 us
  between operations: 13.9 us -> 0.66 us
    dot_general x4 -> x0, matrix products: 97.2 us -> none  [the longest x1 62.7 us: encode_block(): jnp.dot(token_rows, w_in, preferred_element_type=jnp.float32)]
    pallas_call x0 -> x4, Pallas kernels: none -> 82.2 us  [the longest x1 27.2 us: encode(): pl.pallas_call(functools.partial(encode_kernel, block, chunk, shards, sha...]
    gather x1 -> x0, local copies, waits for them, and re-layouts: 76.7 us -> none  [local(): picked = jnp.take(new_index, jnp.where(mine_mask, cand_local, 0), axis=0)]
    unnamed x1 -> x0, blocking collectives: 69.4 us -> none
    psum x1 -> x0, waiting for transfers between devices: 52.7 us -> none  [local(): scores = lax.psum(partial_scores, 'shard')]
    reduce_scatter x1 -> x0, waiting for transfers between devices: 29.3 us -> none  [local(): lax.psum_scatter(weigh_rows(weight_diff, masked_rows), 'shard', scatter_d...]
    dot_general x1 -> x0, other arithmetic: 17.4 us -> none  [local(): jnp.einsum('qd,qkd->qk', queries, masked_rows, preferred_element_type=jnp...]
    scatter x1 -> x0, local copies, waits for them, and re-layouts: 12.4 us -> none  [local(): new_index = old_index.at[local_rows].set(all_fresh, mode='drop')]
  transfers between devices with their start and end apart: 3 -> 0, of which waited for: 2 -> 0; matrix products, arithmetic and copies ran while one was open for 0% -> 0% of each run, Pallas kernels for 0% -> 0%
where the time goes in v1:
time: 87.1 us; the launch traced here: 86.8 us
  Pallas kernels  82.2 us (94%)
  local copies, waits for them, and re-layouts  3.91 us (4%)
    pallas_call x1, Pallas kernels, encode(): pl.pallas_call(functools.partial(encode_kernel, block, chunk, shards, sha...  27.2 us
    pallas_call x1, Pallas kernels, exchange(): pl.pallas_call(functools.partial(exchange_kernel, loaders, shards), out_s...  21.7 us
    pallas_call x1, Pallas kernels, gradient(): pl.pallas_call(functools.partial(grad_kernel, shards), out_shape=[jax.Sha...  21 us
    pallas_call x1, Pallas kernels, score(): pl.pallas_call(functools.partial(score_kernel, tile), out_shape=[jax.Shap...  12.3 us
    unnamed x2, local copies, waits for them, and re-layouts  2.65 us

profile of v1, /device:TPU:1, one launch (start us, length us, event | category | flops | bytes accessed | tf_op | source)
XLA Modules:
  0.0 86.8 jit_solution(10672769822412253324)
XLA Ops:
  0.6 1.3 %reshape.15.gain_ref = f32[1,768]{1,0:T(1,128)} reshape(f32[768]{0:T(1024)} %param.12) | data formatting | bytes 6144 | tf_op jit(solution)/shard_map/reshape | solution.py:98
  1.9 27.2 %encode.1.slots_ref = f32[8,2,896]{2,1,0:T(2,128)} custom-call(bf16[2048,768]{1,0:T(8,128)(2,1)} %x_hbm.1, bf16[768,3072]{1,0:T(8,128)(2,1)} %win_hbm.1, bf16[3072,768]{1,0:T(8,128)(2,1)} %wout_hbm.1, f32[1,768]{1,0:T(1,128)} %reshape.15.gain_ref, s32[8]{0:T(128)} %rows_ref.1), custom_call_target="tpu_custom_call" | custom-call | tf_op jit(solution)/shard_map/encode/pallas_call | solution.py:81
  29.1 21.7 %exchange.1 = bf16[16,16,896]{2,1,0:T(8,128)(2,1)} custom-call(f32[8,2,896]{2,1,0:T(2,128)} %encode.1.slots_ref), custom_call_target="tpu_custom_call" | custom-call | tf_op jit(solution)/shard_map/exchange/pallas_call | solution.py:138
  50.8 12.3 %score.1 = (bf16[4096,768]{1,0:T(8,128)(2,1)}, f32[64,256]{1,0:T(8,128)}, f32[8,256]{1,0:T(8,128)}) custom-call(bf16[256,896]{1,0:T(8,128)(2,1)} %bitcast.4, bf16[256,768]{1,0:T(8,128)(2,1)} %q_ref.1, s32[64,256]{1,0:T(8,128)} %bitcast.5, f32[64,256]{1,0:T(8,128)} %bitcast.7, bf16[4096,768]{1,0:T(8,128)(2,1)} %old_hbm.1), custom_call_target="tpu_custom_call" | custom-call | tf_op jit(solution)/shard_map/score/pallas_call | solution.py:234
  63.1 21.0 %gradient.1 = (f32[1,32]{1,0:T(1,128)}, f32[32,768]{1,0:T(8,128)}) custom-call(f32[64,256]{1,0:T(8,128)} %get-tuple-element.9.score_ref, f32[8,256]{1,0:T(8,128)} %get-tuple-element.10.stats_ref, s32[64,256]{1,0:T(8,128)} %bitcast.6, f32[64,256]{1,0:T(8,128)} %bitcast.8, bf16[4096,768]{1,0:T(8,128)(2,1)} %get-tuple-element.16.new_hbm), custom_call_target="tpu_custom_call" | custom-call | tf_op jit(solution)/shard_map/gradient/pallas_call | solution.py:360
  84.1 1.1 %copy.14 = f32[32]{0:T(128)} copy(f32[32]{0:T(128)} %bitcast.9) | data formatting | bytes 256
  85.2 1.5 %copy.15 = f32[32,768]{1,0:T(8,128)} copy(f32[32,768]{1,0:T(8,128)} %get-tuple-element.18) | data formatting | bytes 196608

commit v2 on v0

v2 whole, which is shorter than its diff:
```python
import functools

import jax
import jax.numpy as jnp
from jax import lax
from jax.experimental import pallas as pl
from jax.experimental.pallas import tpu as pltpu
from jax.sharding import PartitionSpec as P

LEN = 256
EPS = 1e-05
MIB = 2**20
MESH = pl.DeviceIdType.MESH
BF16, F32, I32 = jnp.bfloat16, jnp.float32, jnp.int32
NONE = -1e30


def gelu(v):
    return 0.5 * v * (1.0 + lax.erf(v * 0.7071067811865476))


def main_kernel(block, chunk, loaders, shards,
                x_hbm, win_hbm, wout_hbm, gain_ref, rows_ref, old_hbm, q_ref, cand_ref, teacher_ref,
                loss_ref, grad_ref, fresh_ref, place_ref,
                x, win, wout, inner, mixed, fresh, old, s_all, a_s, hi_s, lo_s, t_map, got, flat, spread, w_s,
                ids, ids_a, ids_b, slots, mine, packed, stats, part, own, inbox,
                load_sem, ids1_send, ids1_recv, ids2_send, ids2_recv,
                send1, recv1, send2, recv2, send3, recv3, send4, recv4):
    tokens, d = x.shape
    ff = win.shape[1]
    rows = old.shape[0]
    k, nq = cand_ref.shape
    per = nq // shards
    blocks, chunks = tokens // block, ff // chunk
    his = rows // 128
    places = loaders * 2 * shards
    ext = his + places // 128
    li, si = lax.axis_index("loader"), lax.axis_index("shard")
    shard_peers = [(li, lax.rem(si + j, shards)) for j in range(1, shards)]
    loader_peers = [(lax.rem(li + j, loaders), si) for j in range(1, loaders)]

    jobs = [pltpu.make_async_copy(src, dst, load_sem.at[i]) for i, (src, dst) in enumerate(
        [(x_hbm, x), (win_hbm, win), (wout_hbm, wout), (old_hbm, old)])]
    for job in jobs[:3]:
        job.start()
    barrier = pltpu.get_barrier_semaphore()
    for peer in shard_peers + loader_peers:
        pl.semaphore_signal(barrier, inc=1, device_id=peer, device_id_type=MESH)

    def send(src, dst, sends, recvs, peers):
        copies = []
        for j, peer in enumerate(peers):
            copy = pltpu.make_async_remote_copy(
                src_ref=src(peer), dst_ref=dst, send_sem=sends.at[j], recv_sem=recvs.at[j],
                device_id=peer, device_id_type=MESH)
            copy.start()
            copies.append(copy)
        return copies

    def arrive(copies):
        for copy in copies:
            copy.wait_recv()

    started = []

    def norm(b):
        for j in range(block // LEN):
            y = mixed[b % 2, j * LEN:(j + 1) * LEN, :]
            centered = y - jnp.mean(y, axis=-1, keepdims=True)
            var = jnp.mean(centered * centered, axis=-1, keepdims=True)
            normed = centered * lax.rsqrt(var + EPS)
            n = b * (block // LEN) + j
            fresh[n:n + 1, :] = jnp.sum(normed, axis=0, keepdims=True) * (1.0 / LEN) * gain_ref[...].reshape(1, d)

    def encode_block(b):
        rs = slice(b * block, (b + 1) * block)
        for c in range(chunks):
            cs = slice(c * chunk, (c + 1) * chunk)
            h = jnp.dot(x[rs, :], win[:, cs], preferred_element_type=F32)
            inner[b % 2, :, cs] = gelu(h).astype(BF16)
            if c == 0 and b > 0:
                norm(b - 1)
        mixed[b % 2] = x[rs, :].astype(F32) + jnp.dot(inner[b % 2], wout[...], preferred_element_type=F32)

    for job in jobs[:3]:
        job.wait()
    jobs[3].start()
    encode_block(0)

    passages = tokens // LEN
    lane8 = lax.broadcasted_iota(I32, (8, 128), 1)
    numbers = [rows_ref[p] for p in range(passages)]
    block_ids = jnp.full((8, 128), -1, I32)
    for p in range(passages):
        block_ids = jnp.where(lane8 == p, numbers[p], block_ids)
    ids[...] = block_ids
    pl.semaphore_wait(barrier, shards + loaders - 2)
    ids_a[si] = block_ids
    sent = send(lambda peer: ids, ids_a.at[si], ids1_send, ids1_recv, shard_peers)
    started += sent
    encode_block(1)
    arrive(sent)
    seen = jnp.concatenate([ids_a[s, 0:1, :] for s in range(shards)], axis=0)
    mine_mask = (seen >= si * rows) & (seen < (si + 1) * rows)
    lane_f = lane8.astype(F32)
    value = (seen - si * rows).astype(F32)
    at0 = jnp.min(jnp.where(mine_mask, lane_f, 999.0), axis=1, keepdims=True)
    at1 = jnp.min(jnp.where(mine_mask & (lane_f != at0), lane_f, 999.0), axis=1, keepdims=True)
    for r, at in enumerate((at0, at1)):
        found = jnp.sum(jnp.where(lane_f == at, value, 0.0), axis=1, keepdims=True)
        ids_b[li, r * shards:(r + 1) * shards, :] = jnp.broadcast_to(jnp.where(at < 900.0, found, -1.0), (8, 128))
    sent = send(lambda peer: ids_b.at[li], ids_b.at[li], ids2_send, ids2_recv, loader_peers)
    started += sent
    for b in range(2, blocks):
        encode_block(b)
    norm(blocks - 1)

    owner = [i // rows for i in numbers]
    slot_iota = lax.broadcasted_iota(I32, (2 * shards, d), 0)
    filled = jnp.zeros((2 * shards, d), F32)
    for p in range(passages):
        rank = sum([(owner[o] == owner[p]).astype(I32) for o in range(p)], jnp.int32(0))
        filled = jnp.where(slot_iota == owner[p] * 2 + rank, fresh[p:p + 1, :], filled)
    for s in range(shards):
        slots[s] = filled[2 * s:2 * s + 2, :]
    mine[si] = slots[si]
    sent_a = send(lambda peer: slots.at[peer[1]], mine.at[si], send1, recv1, shard_peers)
    started += sent_a

    jobs[3].wait()
    tile = 512
    for t in range(rows // tile):
        rs = slice(t * tile, (t + 1) * tile)
        s_all[:, rs] = lax.dot_general(q_ref[...], old[rs, :], (((1,), (1,)), ((), ())), preferred_element_type=F32)

    arrive(sent_a)
    for s in range(shards):
        for r in range(2):
            packed[r * shards + s:r * shards + s + 1, :] = mine[s, r:r + 1, :]
    fresh_ref[li] = packed[...].astype(BF16)
    sent_b = send(lambda peer: fresh_ref.at[li], fresh_ref.at[li], send2, recv2, loader_peers)
    started += sent_b

    arrive(sent)
    where_to = ids_b[...].reshape(places, 128).T[0:8, :]
    place_ref[...] = where_to
    place_i = where_to[0:1, :].astype(I32)
    left = jnp.where(lax.broadcasted_iota(I32, (his, places), 0) == (place_i >> 7),
                     (lax.broadcasted_iota(I32, (his, places), 1) + 1).astype(F32), 0.0).astype(BF16)
    right = jnp.where(lax.broadcasted_iota(I32, (128, places), 0) == (place_i & 127), 1.0, 0.0).astype(BF16)
    t_map[...] = lax.dot_general(left, right, (((1,), (1,)), ((), ())), preferred_element_type=F32)

    local = cand_ref[...] - si * rows
    owned = (local >= 0) & (local < rows)
    high = jnp.where(owned, local >> 7, -1)
    low = local & 127
    hi_s[...] = jnp.concatenate([high, high], axis=0).T
    lo_s[...] = jnp.concatenate([low, low], axis=0).T

    lane = lax.broadcasted_iota(I32, (8, 2 * k), 1)
    sub = lax.broadcasted_iota(I32, (8, 2 * k), 0)
    masks = [lane // k + 2 * v == sub for v in range(4)]

    def pick(g, carry):
        qs = pl.ds(pl.multiple_of(g * 8, 8), 8)
        hi, lo = hi_s[qs, :], lo_s[qs, :]
        out = jnp.zeros((8, 128), F32)
        spot = jnp.zeros((8, 128), F32)
        for h in range(his):
            here = hi == h
            out = jnp.where(here, jnp.take_along_axis(
                s_all[qs, h * 128:(h + 1) * 128], lo, axis=1, mode="promise_in_bounds"), out)
            spot = jnp.where(here, jnp.take_along_axis(
                jnp.broadcast_to(t_map[h:h + 1, :], (8, 128)), lo, axis=1, mode="promise_in_bounds"), spot)
        is_fresh = spot > 0.5
        slot = spot.astype(I32) - 1
        hi = jnp.where(is_fresh, his + (slot >> 7), hi)
        lo = jnp.where(is_fresh, slot & 127, lo)
        hi_s[qs, :] = hi
        lo_s[qs, :] = lo
        got[qs, :] = out
        lo_f = lo.astype(F32)
        flat[g] = jnp.broadcast_to(jnp.concatenate(
            [jnp.sum(jnp.where(m, lo_f, 0.0), axis=0, keepdims=True) for m in masks], axis=1), (8, 8 * k))
        wide = jnp.concatenate([jnp.where(m, hi, -1) for m in masks], axis=1)
        a_s[g] = jnp.concatenate([jnp.where(wide == h, 1.0, 0.0) for h in range(ext)], axis=0).astype(BF16)
        return carry

    lax.fori_loop(0, nq // 8, pick, 0)
    teacher = teacher_ref[...]
    shifted = teacher - jnp.max(teacher, axis=0, keepdims=True)
    log_t = shifted - jnp.log(jnp.sum(jnp.exp(shifted), axis=0, keepdims=True))
    p_t = jnp.exp(log_t)
    entropy = jnp.sum(p_t * log_t, axis=0, keepdims=True)

    arrive(sent_b)
    rows_f = fresh_ref[...].reshape(places, d)
    s_fresh = lax.dot_general(q_ref[...], rows_f, (((1,), (1,)), ((), ())), preferred_element_type=F32)
    s_all[:, 0:places] = s_fresh

    def pick_fresh(g, carry):
        qs = pl.ds(pl.multiple_of(g * 8, 8), 8)
        hi, lo = hi_s[qs, :], lo_s[qs, :]
        out = got[qs, :]
        for h in range(places // 128):
            out = jnp.where(hi == his + h, jnp.take_along_axis(
                s_all[qs, h * 128:(h + 1) * 128], lo, axis=1, mode="promise_in_bounds"), out)
        got[qs, :] = out
        return carry

    lax.fori_loop(0, nq // 8, pick_fresh, 0)
    score = got[...].T[0:k, :]
    top = jnp.max(jnp.where(owned, score, NONE), axis=0, keepdims=True)
    diff = score - top
    z = jnp.sum(jnp.where(owned, jnp.exp(jnp.where(owned, diff, 0.0)), 0.0), axis=0, keepdims=True)
    a = jnp.sum(jnp.where(owned, p_t * diff, 0.0), axis=0, keepdims=True)
    b = jnp.sum(jnp.where(owned, p_t, 0.0), axis=0, keepdims=True)
    stats[si] = jnp.concatenate([top, z, a, b, top, z, a, b], axis=0)
    sent_s = send(lambda peer: stats.at[si], stats.at[si], send3, recv3, shard_peers)
    started += sent_s
    arrive(sent_s)
    every = [stats[s] for s in range(shards)]
    top = functools.reduce(jnp.maximum, [e[0:1] for e in every])
    z = sum([e[1:2] * jnp.exp(e[0:1] - top) for e in every])
    cross = sum([e[2:3] + e[3:4] * (e[0:1] - top) for e in every])
    log_z = jnp.log(z)
    loss = entropy - cross + log_z
    out = jnp.zeros((1, per), F32)
    for s in range(shards):
        out = jnp.where(si == s, loss[:, s * per:(s + 1) * per], out)
    loss_ref[...] = out
    student = jnp.exp(jnp.where(owned, score - top - log_z, 0.0))
    weight = jnp.where(owned, student - p_t, 0.0).astype(BF16).astype(F32)
    w_s[...] = jnp.concatenate([weight, weight], axis=0).T

    lo_iota = lax.broadcasted_iota(I32, (128, 8 * k), 0).astype(F32)

    def group(g):
        w2 = w_s[pl.ds(pl.multiple_of(g * 8, 8), 8), :]
        w_flat = jnp.concatenate(
            [jnp.sum(jnp.where(m, w2, 0.0), axis=0, keepdims=True) for m in masks], axis=1)
        right = jnp.where(lo_iota == flat[g][0:1, :], w_flat, 0.0).astype(BF16)
        return lax.dot_general(a_s[g], right, (((1,), (1,)), ((), ())), preferred_element_type=F32)

    def place(g, carry):
        one, two = group(g * 2), group(g * 2 + 1)
        qs = pl.ds(pl.multiple_of(g * 16, 16), 16)
        for h in range(ext):
            both = jnp.concatenate([one[h * 8:(h + 1) * 8], two[h * 8:(h + 1) * 8]], axis=0)
            spread[qs, h * 128:(h + 1) * 128] = both.astype(BF16)
        return carry

    lax.fori_loop(0, nq // 16, place, 0)
    total = (jnp.dot(spread[:, 0:rows], old[...], preferred_element_type=F32)
             + jnp.dot(spread[:, rows:rows + places], fresh_ref[...].reshape(places, d), preferred_element_type=F32))
    own_block = jnp.zeros((per, d), F32)
    for s in range(shards):
        piece = total[s * per:(s + 1) * per, :]
        part[s] = piece.astype(BF16)
        own_block = jnp.where(si == s, piece, own_block)
    own[...] = own_block
    sent_g = []
    for j, peer in enumerate(shard_peers):
        copy = pltpu.make_async_remote_copy(
            src_ref=part.at[peer[1]], dst_ref=inbox.at[j], send_sem=send4.at[j], recv_sem=recv4.at[j],
            device_id=peer, device_id_type=MESH)
        copy.start()
        sent_g.append(copy)
    acc = own[...]
    for j, copy in enumerate(sent_g):
        copy.wait_recv()
        acc = acc + inbox[j].astype(F32)
    grad_ref[...] = acc
    for copy in started + sent_g:
        copy.wait_send()


def main(loaders, shards, hidden, w_in, w_out, gain, passage_rows, old_index, queries, cand_t, teacher_t):
    tokens, d = hidden.shape
    ff = w_in.shape[1]
    rows = old_index.shape[0]
    k, nq = cand_t.shape
    per = nq // shards
    places = loaders * 2 * shards
    ext = (rows + places) // 128
    block, chunk = 512, 768
    anywhere = pl.BlockSpec(memory_space=pl.ANY)
    vmem = pl.BlockSpec(memory_space=pltpu.VMEM)
    smem = pl.BlockSpec(memory_space=pltpu.SMEM)
    dma = pltpu.SemaphoreType.DMA
    return pl.pallas_call(
        functools.partial(main_kernel, block, chunk, loaders, shards),
        out_shape=[
            jax.ShapeDtypeStruct((1, per), F32),
            jax.ShapeDtypeStruct((per, d), F32),
            jax.ShapeDtypeStruct((loaders, 2 * shards, d), BF16),
            jax.ShapeDtypeStruct((8, places), F32),
        ],
        in_specs=[anywhere] * 3 + [vmem, smem, anywhere, vmem, vmem, vmem],
        out_specs=[vmem] * 4,
        scratch_shapes=[
            pltpu.VMEM((tokens, d), BF16),
            pltpu.VMEM((d, ff), BF16),
            pltpu.VMEM((ff, d), BF16),
            pltpu.VMEM((2, block, ff), BF16),
            pltpu.VMEM((2, block, d), F32),
            pltpu.VMEM((tokens // LEN, d), F32),
            pltpu.VMEM((rows, d), BF16),
            pltpu.VMEM((nq, rows), F32),
            pltpu.VMEM((nq // 8, 8 * ext, 8 * k), BF16),
            pltpu.VMEM((nq, 2 * k), I32),
            pltpu.VMEM((nq, 2 * k), I32),
            pltpu.VMEM((rows // 128, 128), F32),
            pltpu.VMEM((nq, 2 * k), F32),
            pltpu.VMEM((nq // 8, 8, 8 * k), F32),
            pltpu.VMEM((nq, 128 * ext), BF16),
            pltpu.VMEM((nq, 2 * k), F32),
            pltpu.VMEM((8, 128), I32),
            pltpu.VMEM((shards, 8, 128), I32),
            pltpu.VMEM((loaders, 2 * shards, 128), F32),
            pltpu.VMEM((shards, 2, d), F32),
            pltpu.VMEM((shards, 2, d), F32),
            pltpu.VMEM((2 * shards, d), F32),
            pltpu.VMEM((shards, 8, nq), F32),
            pltpu.VMEM((shards, per, d), BF16),
            pltpu.VMEM((per, d), F32),
            pltpu.VMEM((shards, per, d), BF16),
            dma((4,)),
            dma((shards,)), dma((shards,)), dma((loaders,)), dma((loaders,)),
            dma((shards,)), dma((shards,)), dma((loaders,)), dma((loaders,)),
            dma((shards,)), dma((shards,)), dma((shards,)), dma((shards,)),
        ],
        compiler_params=pltpu.CompilerParams(collective_id=0, has_side_effects=True, vmem_limit_bytes=60 * MIB),
        name="main",
    )(hidden, w_in, w_out, gain, passage_rows, old_index, queries, cand_t, teacher_t)


def index_kernel(tile, fresh_ref, place_ref, loss_in, grad_in, old_hbm, new_hbm, loss_out, grad_out,
                 old, new, in_sem, out_sem):
    rows, d = old.shape
    tiles = rows // tile
    loads = [pltpu.make_async_copy(old_hbm.at[pl.ds(t * tile, tile)], old.at[pl.ds(t * tile, tile)], in_sem.at[t])
             for t in range(tiles)]
    for load in loads:
        load.start()
    loss_out[...] = loss_in[...]
    grad_out[...] = grad_in[...]
    where_to = place_ref[0:1, :].astype(I32)
    places = fresh_ref.shape[0]
    ones = jnp.ones((places, 128), BF16)
    row_iota = lax.broadcasted_iota(I32, (tile, places), 0)
    stores = []
    for t in range(tiles):
        rs = slice(t * tile, (t + 1) * tile)
        place = jnp.where(row_iota + t * tile == where_to, 1.0, 0.0).astype(BF16)
        put = jnp.dot(place, fresh_ref[...], preferred_element_type=F32)
        has = jnp.dot(place, ones, preferred_element_type=F32)
        loads[t].wait()
        for c in range(d // 128):
            cs = slice(c * 128, (c + 1) * 128)
            new[rs, cs] = jnp.where(has > 0.5, put[:, cs], old[rs, cs].astype(F32)).astype(BF16)
        store = pltpu.make_async_copy(new.at[pl.ds(t * tile, tile)], new_hbm.at[pl.ds(t * tile, tile)], out_sem.at[t])
        store.start()
        stores.append(store)
    for store in stores:
        store.wait()


def refresh(fresh, places, loss, grad, old_index):
    rows, d = old_index.shape
    tile = 512
    anywhere = pl.BlockSpec(memory_space=pl.ANY)
    vmem = pl.BlockSpec(memory_space=pltpu.VMEM)
    return pl.pallas_call(
        functools.partial(index_kernel, tile),
        out_shape=[jax.ShapeDtypeStruct((rows, d), BF16), jax.ShapeDtypeStruct(loss.shape, F32),
                   jax.ShapeDtypeStruct(grad.shape, F32)],
        in_specs=[vmem] * 4 + [anywhere],
        out_specs=[anywhere, vmem, vmem],
        scratch_shapes=[
            pltpu.VMEM((rows, d), BF16),
            pltpu.VMEM((rows, d), BF16),
            pltpu.SemaphoreType.DMA((rows // tile,)),
            pltpu.SemaphoreType.DMA((rows // tile,)),
        ],
        compiler_params=pltpu.CompilerParams(vmem_limit_bytes=48 * MIB),
        name="refresh",
    )(fresh, places, loss, grad, old_index)


def solution(mesh):
    loaders, shards = mesh.shape["loader"], mesh.shape["shard"]

    def local(hidden_states, w_in, w_out, ln_gain, passage_rows, old_index, queries, candidates, teacher):
        cand_t, teacher_t = candidates.T, teacher.T
        loss, grad, fresh, places = main(
            loaders, shards, hidden_states, w_in, w_out, ln_gain, passage_rows, old_index, queries, cand_t, teacher_t)
        new_index, loss, grad = refresh(fresh.reshape(-1, fresh.shape[-1]), places, loss, grad, old_index)
        return new_index, loss.reshape(-1), grad

    return jax.shard_map(
        local,
        mesh=mesh,
        in_specs=(
            P(("loader", "shard"), None),
            P(),
            P(),
            P(),
            P(("loader", "shard")),
            P("shard", None),
            P("loader", None),
            P("loader", None),
            P("loader", None),
        ),
        out_specs=(P("shard", None), P(("loader", "shard")), P(("loader", "shard"), None)),
        check_vma=False,
    )
```

time: 386 us -> 79.4 us (0.21)
  matrix products: 97.2 us -> 0 us
  local copies, waits for them, and re-layouts: 98.1 us -> 3.24 us
  waiting for transfers between devices: 82.1 us -> 0 us
  Pallas kernels: 0 us -> 75.1 us
  blocking collectives: 69.4 us -> 0 us
  other arithmetic: 22.8 us -> 0 us
  between operations: 13.9 us -> 0.83 us
    dot_general x4 -> x0, matrix products: 97.2 us -> none  [the longest x1 62.7 us: encode_block(): jnp.dot(token_rows, w_in, preferred_element_type=jnp.float32)]
    gather x1 -> x0, local copies, waits for them, and re-layouts: 76.7 us -> none  [local(): picked = jnp.take(new_index, jnp.where(mine_mask, cand_local, 0), axis=0)]
    pallas_call x0 -> x2, Pallas kernels: none -> 75.1 us  [the longest x1 67 us: main(): pl.pallas_call(functools.partial(main_kernel, block, chunk, loaders, shar...]
    unnamed x1 -> x0, blocking collectives: 69.4 us -> none
    psum x1 -> x0, waiting for transfers between devices: 52.7 us -> none  [local(): scores = lax.psum(partial_scores, 'shard')]
    reduce_scatter x1 -> x0, waiting for transfers between devices: 29.3 us -> none  [local(): lax.psum_scatter(weigh_rows(weight_diff, masked_rows), 'shard', scatter_d...]
    dot_general x1 -> x0, other arithmetic: 17.4 us -> none  [local(): jnp.einsum('qd,qkd->qk', queries, masked_rows, preferred_element_type=jnp...]
    scatter x1 -> x0, local copies, waits for them, and re-layouts: 12.4 us -> none  [local(): new_index = old_index.at[local_rows].set(all_fresh, mode='drop')]
  transfers between devices with their start and end apart: 3 -> 0, of which waited for: 2 -> 0; matrix products, arithmetic and copies ran while one was open for 0% -> 0% of each run, Pallas kernels for 0% -> 0%
where the time goes in v2:
time: 79.4 us; the launch traced here: 79.1 us
  Pallas kernels  75.1 us (95%)
  local copies, waits for them, and re-layouts  3.24 us (4%)
  between operations  0.83 us (1%)
    pallas_call x1, Pallas kernels, main(): pl.pallas_call(functools.partial(main_kernel, block, chunk, loaders, shar...  67 us
    pallas_call x1, Pallas kernels, refresh(): pl.pallas_call(functools.partial(index_kernel, tile), out_shape=[jax.Shap...  8.02 us
    unnamed x8, local copies, waits for them, and re-layouts  3.24 us

profile of v2, /device:TPU:1, one launch (start us, length us, event | category | flops | bytes accessed | tf_op | source)
XLA Modules:
  0.0 79.1 jit_solution(1024706541243876390)
XLA Ops:
  0.6 67.0 %main.1 = (f32[1,32]{1,0:T(1,128)}, f32[32,768]{1,0:T(8,128)}, bf16[16,16,768]{2,1,0:T(8,128)(2,1)}, f32[8,256]{1,0:T(8,128)}) custom-call(bf16[2048,768]{1,0:T(8,128)(2,1)} %x_hbm.1, bf16[768,3072]{1,0:T(8,128)(2,1)} %win_hbm.1, bf16[3072,768]{1,0:T(8,128)(2,1)} %wout_hbm.1, f32[768]{0:T(1024)} %gain_ref.1, s32[8]{0:T(128)} %rows_ref.1, ...), custom_call_target="tpu_custom_call" | custom-call | tf_op jit(solution)/shard_map/main/pallas_call | solution.py:291
  67.7 0.0 copy-start
  67.7 1.0 %copy-done = bf16[16,16,768]{2,1,0:T(8,128)(2,1)S(1)} copy-done((bf16[16,16,768]{2,1,0:T(8,128)(2,1)S(1)}, bf16[16,16,768]{2,1,0:T(8,128)(2,1)}, u32[]{:S(2)}) %copy-start) | copy-done | bytes 393240
  68.7 0.0 copy-start.1
  68.7 0.9 %copy-done.1 = f32[32,768]{1,0:T(8,128)S(1)} copy-done((f32[32,768]{1,0:T(8,128)S(1)}, f32[32,768]{1,0:T(8,128)}, u32[]{:S(2)}) %copy-start.1) | copy-done | bytes 98328
  69.6 0.0 copy-start.2
  69.6 0.7 copy-done.2
  70.3 0.0 copy-start.3
  70.3 0.7 copy-done.3
  70.9 8.0 %refresh.1 = (bf16[4096,768]{1,0:T(8,128)(2,1)}, f32[1,32]{1,0:T(1,128)}, f32[32,768]{1,0:T(8,128)}) custom-call(bf16[256,768]{1,0:T(8,128)(2,1)S(1)} %bitcast.4, f32[8,256]{1,0:T(8,128)S(1)} %copy-done.2, f32[1,32]{1,0:T(1,128)S(1)} %copy-done.3, f32[32,768]{1,0:T(8,128)S(1)} %copy-done.1, bf16[4096,768]{1,0:T(8,128)(2,1)} %old_hbm.3), custom_call_target="tpu_custom_call" | custom-call | tf_op jit(solution)/shard_map/refresh/pallas_call | solution.py:374
Async XLA Ops:
  67.7 1.0 %copy-start = (bf16[16,16,768]{2,1,0:T(8,128)(2,1)S(1)}, bf16[16,16,768]{2,1,0:T(8,128)(2,1)}, u32[]{:S(2)}) copy-start(bf16[16,16,768]{2,1,0:T(8,128)(2,1)} %get-tuple-element.10) | copy-start | bytes 1179652
  68.7 0.9 %copy-start.1 = (f32[32,768]{1,0:T(8,128)S(1)}, f32[32,768]{1,0:T(8,128)}, u32[]{:S(2)}) copy-start(f32[32,768]{1,0:T(8,128)} %get-tuple-element.13.grad_in) | copy-start | bytes 294916
  69.6 0.7 copy-start.2
  70.3 0.7 copy-start.3

commit v3 on v2

--- a/solution.py
+++ b/solution.py
@@ -23,9 +23,9 @@
                 x_hbm, win_hbm, wout_hbm, gain_ref, rows_ref, old_hbm, q_ref, cand_ref, teacher_ref,
                 loss_ref, grad_ref, fresh_ref, place_ref,
                 x, win, wout, inner, mixed, fresh, old, s_all, a_s, hi_s, lo_s, t_map, got, flat, spread, w_s,
-                ids, ids_a, ids_b, slots, mine, packed, stats, part, own, inbox,
+                ids, ids_a, ids_b, slots, mine, packed, stats, tot, pair, part, own, inbox,
                 load_sem, ids1_send, ids1_recv, ids2_send, ids2_recv,
-                send1, recv1, send2, recv2, send3, recv3, send4, recv4):
+                send1, recv1, send2, recv2, send3, recv3, send4, recv4, send5, recv5):
     tokens, d = x.shape
     ff = win.shape[1]
     rows = old.shape[0]
@@ -39,9 +39,14 @@
     shard_peers = [(li, lax.rem(si + j, shards)) for j in range(1, shards)]
     loader_peers = [(lax.rem(li + j, loaders), si) for j in range(1, loaders)]
 
-    jobs = [pltpu.make_async_copy(src, dst, load_sem.at[i]) for i, (src, dst) in enumerate(
-        [(x_hbm, x), (win_hbm, win), (wout_hbm, wout), (old_hbm, old)])]
-    for job in jobs[:3]:
+    half, head = ff // 2, pl.ds(0, block)
+    rest = pl.ds(block, tokens - block)
+    jobs = [pltpu.make_async_copy(src, dst, load_sem.at[i]) for i, (src, dst) in enumerate([
+        (x_hbm.at[head], x.at[head]),
+        (win_hbm.at[:, pl.ds(0, half)], win.at[:, pl.ds(0, half)]),
+        (win_hbm.at[:, pl.ds(half, half)], win.at[:, pl.ds(half, half)]),
+        (wout_hbm, wout), (x_hbm.at[rest], x.at[rest]), (old_hbm, old)])]
+    for job in jobs[:5]:
         job.start()
     barrier = pltpu.get_barrier_semaphore()
     for peer in shard_peers + loader_peers:
@@ -76,16 +81,21 @@
         rs = slice(b * block, (b + 1) * block)
         for c in range(chunks):
             cs = slice(c * chunk, (c + 1) * chunk)
+            if b == 0 and c * chunk == half:
+                jobs[2].wait()
             h = jnp.dot(x[rs, :], win[:, cs], preferred_element_type=F32)
             inner[b % 2, :, cs] = gelu(h).astype(BF16)
             if c == 0 and b > 0:
                 norm(b - 1)
+        if b == 0:
+            jobs[3].wait()
+            jobs[4].wait()
         mixed[b % 2] = x[rs, :].astype(F32) + jnp.dot(inner[b % 2], wout[...], preferred_element_type=F32)
 
-    for job in jobs[:3]:
-        job.wait()
-    jobs[3].start()
+    jobs[0].wait()
+    jobs[1].wait()
     encode_block(0)
+    jobs[5].start()
 
     passages = tokens // LEN
     lane8 = lax.broadcasted_iota(I32, (8, 128), 1)
@@ -127,7 +137,7 @@
     sent_a = send(lambda peer: slots.at[peer[1]], mine.at[si], send1, recv1, shard_peers)
     started += sent_a
 
-    jobs[3].wait()
+    jobs[5].wait()
     tile = 512
     for t in range(rows // tile):
         rs = slice(t * tile, (t + 1) * tile)
@@ -208,7 +218,7 @@
         got[qs, :] = out
         return carry
 
-    lax.fori_loop(0, nq // 8, pick_fresh, 0)
+    lax.fori_loop(0, nq // 8, pick_fresh, 0, unroll=8)
     score = got[...].T[0:k, :]
     top = jnp.max(jnp.where(owned, score, NONE), axis=0, keepdims=True)
     diff = score - top
@@ -250,27 +260,51 @@
             spread[qs, h * 128:(h + 1) * 128] = both.astype(BF16)
         return carry
 
-    lax.fori_loop(0, nq // 16, place, 0)
-    total = (jnp.dot(spread[:, 0:rows], old[...], preferred_element_type=F32)
-             + jnp.dot(spread[:, rows:rows + places], fresh_ref[...].reshape(places, d), preferred_element_type=F32))
-    own_block = jnp.zeros((per, d), F32)
-    for s in range(shards):
-        piece = total[s * per:(s + 1) * per, :]
-        part[s] = piece.astype(BF16)
-        own_block = jnp.where(si == s, piece, own_block)
-    own[...] = own_block
-    sent_g = []
-    for j, peer in enumerate(shard_peers):
+    lax.fori_loop(0, nq // 16, place, 0, unroll=4)
+    core, y = lax.rem(si, 2), si // 2
+    ys = shards // 2
+    mate = (li, 2 * y + 1 - core)
+    wide = d // 2
+
+    def partial(c):
+        cs = slice(c * wide, (c + 1) * wide)
+        total = (jnp.dot(spread[:, 0:rows], old[:, cs], preferred_element_type=F32)
+                 + jnp.dot(spread[:, rows:rows + places], fresh_ref[...].reshape(places, d)[:, cs],
+                           preferred_element_type=F32))
+        for s in range(shards):
+            tot[c, s % 2, s // 2] = total[s * per:(s + 1) * per, :]
         copy = pltpu.make_async_remote_copy(
-            src_ref=part.at[peer[1]], dst_ref=inbox.at[j], send_sem=send4.at[j], recv_sem=recv4.at[j],
-            device_id=peer, device_id_type=MESH)
+            src_ref=tot.at[c, 1 - core], dst_ref=pair.at[c], send_sem=send5.at[c], recv_sem=recv5.at[c],
+            device_id=mate, device_id_type=MESH)
         copy.start()
-        sent_g.append(copy)
-    acc = own[...]
-    for j, copy in enumerate(sent_g):
+        return copy
+
+    def pass_on(c, copy):
         copy.wait_recv()
-        acc = acc + inbox[j].astype(F32)
-    grad_ref[...] = acc
+        for t in range(ys):
+            part[c, t] = (tot[c, core, t] + pair[c, t]).astype(BF16)
+        copies = []
+        for j in range(1, ys):
+            to = lax.rem(y + j, ys)
+            copy = pltpu.make_async_remote_copy(
+                src_ref=part.at[c, to], dst_ref=inbox.at[c, j - 1], send_sem=send4.at[c, j - 1],
+                recv_sem=recv4.at[c, j - 1], device_id=(li, 2 * to + core), device_id_type=MESH)
+            copy.start()
+            copies.append(copy)
+        own[c] = tot[c, core, y] + pair[c, y]
+        return copies
+
+    first = partial(0)
+    second = partial(1)
+    sent_0 = pass_on(0, first)
+    sent_1 = pass_on(1, second)
+    for c, copies in enumerate((sent_0, sent_1)):
+        acc = own[c]
+        for j, copy in enumerate(copies):
+            copy.wait_recv()
+            acc = acc + inbox[c, j].astype(F32)
+        grad_ref[:, c * wide:(c + 1) * wide] = acc
+    sent_g = [first, second] + sent_0 + sent_1
     for copy in started + sent_g:
         copy.wait_send()
 
@@ -322,29 +356,33 @@
             pltpu.VMEM((shards, 2, d), F32),
             pltpu.VMEM((2 * shards, d), F32),
             pltpu.VMEM((shards, 8, nq), F32),
-            pltpu.VMEM((shards, per, d), BF16),
-            pltpu.VMEM((per, d), F32),
-            pltpu.VMEM((shards, per, d), BF16),
-            dma((4,)),
+            pltpu.VMEM((2, 2, shards // 2, per, d // 2), F32),
+            pltpu.VMEM((2, shards // 2, per, d // 2), F32),
+            pltpu.VMEM((2, shards // 2, per, d // 2), BF16),
+            pltpu.VMEM((2, per, d // 2), F32),
+            pltpu.VMEM((2, shards // 2, per, d // 2), BF16),
+            dma((6,)),
             dma((shards,)), dma((shards,)), dma((loaders,)), dma((loaders,)),
             dma((shards,)), dma((shards,)), dma((loaders,)), dma((loaders,)),
-            dma((shards,)), dma((shards,)), dma((shards,)), dma((shards,)),
+            dma((shards,)), dma((shards,)), dma((2, shards)), dma((2, shards)), dma((2,)), dma((2,)),
         ],
         compiler_params=pltpu.CompilerParams(collective_id=0, has_side_effects=True, vmem_limit_bytes=60 * MIB),
         name="main",
     )(hidden, w_in, w_out, gain, passage_rows, old_index, queries, cand_t, teacher_t)
 
 
-def index_kernel(tile, fresh_ref, place_ref, loss_in, grad_in, old_hbm, new_hbm, loss_out, grad_out,
-                 old, new, in_sem, out_sem):
+def index_kernel(tile, fresh_hbm, place_hbm, loss_hbm, grad_hbm, old_hbm, new_hbm, loss_out, grad_out,
+                 fresh_ref, place_ref, old, new, side_sem, in_sem, out_sem):
     rows, d = old.shape
     tiles = rows // tile
+    sides = [pltpu.make_async_copy(src, dst, side_sem.at[i]) for i, (src, dst) in enumerate(
+        [(place_hbm, place_ref), (fresh_hbm, fresh_ref), (loss_hbm, loss_out), (grad_hbm, grad_out)])]
     loads = [pltpu.make_async_copy(old_hbm.at[pl.ds(t * tile, tile)], old.at[pl.ds(t * tile, tile)], in_sem.at[t])
              for t in range(tiles)]
-    for load in loads:
+    for load in sides[0:2] + loads + sides[2:4]:
         load.start()
-    loss_out[...] = loss_in[...]
-    grad_out[...] = grad_in[...]
+    sides[0].wait()
+    sides[1].wait()
     where_to = place_ref[0:1, :].astype(I32)
     places = fresh_ref.shape[0]
     ones = jnp.ones((places, 128), BF16)
@@ -362,7 +400,7 @@
         store = pltpu.make_async_copy(new.at[pl.ds(t * tile, tile)], new_hbm.at[pl.ds(t * tile, tile)], out_sem.at[t])
         store.start()
         stores.append(store)
-    for store in stores:
+    for store in stores + sides[2:4]:
         store.wait()
 
 
@@ -370,20 +408,22 @@
     rows, d = old_index.shape
     tile = 512
     anywhere = pl.BlockSpec(memory_space=pl.ANY)
-    vmem = pl.BlockSpec(memory_space=pltpu.VMEM)
     return pl.pallas_call(
         functools.partial(index_kernel, tile),
         out_shape=[jax.ShapeDtypeStruct((rows, d), BF16), jax.ShapeDtypeStruct(loss.shape, F32),
                    jax.ShapeDtypeStruct(grad.shape, F32)],
-        in_specs=[vmem] * 4 + [anywhere],
-        out_specs=[anywhere, vmem, vmem],
+        in_specs=[anywhere] * 5,
+        out_specs=[anywhere] * 3,
         scratch_shapes=[
+            pltpu.VMEM(fresh.shape, BF16),
+            pltpu.VMEM(places.shape, F32),
             pltpu.VMEM((rows, d), BF16),
             pltpu.VMEM((rows, d), BF16),
+            pltpu.SemaphoreType.DMA((4,)),
             pltpu.SemaphoreType.DMA((rows // tile,)),
             pltpu.SemaphoreType.DMA((rows // tile,)),
         ],
-        compiler_params=pltpu.CompilerParams(vmem_limit_bytes=48 * MIB),
+        compiler_params=pltpu.CompilerParams(vmem_limit_bytes=60 * MIB),
         name="refresh",
     )(fresh, places, loss, grad, old_index)
 

time: 79.4 us -> 69.9 us (0.88)
  Pallas kernels: 75.1 us -> 69 us
  local copies, waits for them, and re-layouts: 3.24 us -> 0 us
    pallas_call x1, Pallas kernels: 67 us -> 59.6 us  [main(): pl.pallas_call(functools.partial(main_kernel, block, chunk, loaders, shar...]
    unnamed x8 -> x0, local copies, waits for them, and re-layouts: 3.24 us -> none
    pallas_call x1, Pallas kernels: 8.02 us -> 9.34 us  [refresh(): pl.pallas_call(functools.partial(index_kernel, tile), out_shape=[jax.Shap...]
where the time goes in v3:
time: 69.9 us; the launch traced here: 69.8 us
  Pallas kernels  69 us (99%)
  between operations  0.82 us (1%)
    pallas_call x1, Pallas kernels, main(): pl.pallas_call(functools.partial(main_kernel, block, chunk, loaders, shar...  59.6 us
    pallas_call x1, Pallas kernels, refresh(): pl.pallas_call(functools.partial(index_kernel, tile), out_shape=[jax.Shap...  9.34 us

profile of v3, /device:TPU:1, one launch (start us, length us, event | category | flops | bytes accessed | tf_op | source)
XLA Modules:
  0.0 69.8 jit_solution(9903878423556265977)
XLA Ops:
  0.6 59.6 %main.1 = (f32[1,32]{1,0:T(1,128)}, f32[32,768]{1,0:T(8,128)}, bf16[16,16,768]{2,1,0:T(8,128)(2,1)}, f32[8,256]{1,0:T(8,128)}) custom-call(bf16[2048,768]{1,0:T(8,128)(2,1)} %x_hbm.1, bf16[768,3072]{1,0:T(8,128)(2,1)} %win_hbm.1, bf16[3072,768]{1,0:T(8,128)(2,1)} %wout_hbm.1, f32[768]{0:T(1024)} %gain_ref.1, s32[8]{0:T(128)} %rows_ref.1, ...), custom_call_target="tpu_custom_call" | custom-call | tf_op jit(solution)/shard_map/main/pallas_call | solution.py:325
  60.3 9.3 %refresh.1 = (bf16[4096,768]{1,0:T(8,128)(2,1)}, f32[1,32]{1,0:T(1,128)}, f32[32,768]{1,0:T(8,128)}) custom-call(bf16[256,768]{1,0:T(8,128)(2,1)} %bitcast.4, f32[8,256]{1,0:T(8,128)} %get-tuple-element.11.place_hbm, f32[1,32]{1,0:T(1,128)} %get-tuple-element.12.loss_hbm, f32[32,768]{1,0:T(8,128)} %get-tuple-element.13.grad_hbm, bf16[4096,768]{1,0:T(8,128)(2,1)} %old_hbm.3), custom_call_target="tpu_custom_call" | custom-call | tf_op jit(solution)/shard_map/refresh/pallas_call | solution.py:411

commit v4 on v3

--- a/solution.py
+++ b/solution.py
@@ -21,8 +21,8 @@
 
 def main_kernel(block, chunk, loaders, shards,
                 x_hbm, win_hbm, wout_hbm, gain_ref, rows_ref, old_hbm, q_ref, cand_ref, teacher_ref,
-                loss_ref, grad_ref, fresh_ref, place_ref,
-                x, win, wout, inner, mixed, fresh, old, s_all, a_s, hi_s, lo_s, t_map, got, flat, spread, w_s,
+                loss_ref, grad_ref, old,
+                x, win, wout, inner, mixed, fresh, fresh_ref, s_all, a_s, hi_s, lo_s, t_map, got, r_s, spread, w_s,
                 ids, ids_a, ids_b, slots, mine, packed, stats, tot, pair, part, own, inbox,
                 load_sem, ids1_send, ids1_recv, ids2_send, ids2_recv,
                 send1, recv1, send2, recv2, send3, recv3, send4, recv4, send5, recv5):
@@ -34,7 +34,8 @@
     blocks, chunks = tokens // block, ff // chunk
     his = rows // 128
     places = loaders * 2 * shards
-    ext = his + places // 128
+    ext = (rows + places) // 256
+    pads = ext + ext % 2
     li, si = lax.axis_index("loader"), lax.axis_index("shard")
     shard_peers = [(li, lax.rem(si + j, shards)) for j in range(1, shards)]
     loader_peers = [(lax.rem(li + j, loaders), si) for j in range(1, loaders)]
@@ -153,7 +154,6 @@
 
     arrive(sent)
     where_to = ids_b[...].reshape(places, 128).T[0:8, :]
-    place_ref[...] = where_to
     place_i = where_to[0:1, :].astype(I32)
     left = jnp.where(lax.broadcasted_iota(I32, (his, places), 0) == (place_i >> 7),
                      (lax.broadcasted_iota(I32, (his, places), 1) + 1).astype(F32), 0.0).astype(BF16)
@@ -170,6 +170,8 @@
     lane = lax.broadcasted_iota(I32, (8, 2 * k), 1)
     sub = lax.broadcasted_iota(I32, (8, 2 * k), 0)
     masks = [lane // k + 2 * v == sub for v in range(4)]
+
+    lo_iota = lax.broadcasted_iota(I32, (256, 8 * k), 0).astype(F32)
 
     def pick(g, carry):
         qs = pl.ds(pl.multiple_of(g * 8, 8), 8)
@@ -189,11 +191,12 @@
         hi_s[qs, :] = hi
         lo_s[qs, :] = lo
         got[qs, :] = out
-        lo_f = lo.astype(F32)
-        flat[g] = jnp.broadcast_to(jnp.concatenate(
-            [jnp.sum(jnp.where(m, lo_f, 0.0), axis=0, keepdims=True) for m in masks], axis=1), (8, 8 * k))
-        wide = jnp.concatenate([jnp.where(m, hi, -1) for m in masks], axis=1)
-        a_s[g] = jnp.concatenate([jnp.where(wide == h, 1.0, 0.0) for h in range(ext)], axis=0).astype(BF16)
+        lo_f = (lo + (hi & 1) * 128).astype(F32)
+        low_flat = jnp.concatenate(
+            [jnp.sum(jnp.where(m, lo_f, 0.0), axis=0, keepdims=True) for m in masks], axis=1)
+        r_s[g] = jnp.where(lo_iota == low_flat, 1.0, 0.0).astype(BF16)
+        wide = jnp.concatenate([jnp.where(m, hi >> 1, -1) for m in masks], axis=1)
+        a_s[g] = jnp.concatenate([jnp.where(wide == h, 1.0, 0.0) for h in range(pads)], axis=0).astype(BF16)
         return carry
 
     lax.fori_loop(0, nq // 8, pick, 0)
@@ -218,7 +221,7 @@
         got[qs, :] = out
         return carry
 
-    lax.fori_loop(0, nq // 8, pick_fresh, 0, unroll=8)
+    lax.fori_loop(0, nq // 8, pick_fresh, 0, unroll=16)
     score = got[...].T[0:k, :]
     top = jnp.max(jnp.where(owned, score, NONE), axis=0, keepdims=True)
     diff = score - top
@@ -243,21 +246,20 @@
     weight = jnp.where(owned, student - p_t, 0.0).astype(BF16).astype(F32)
     w_s[...] = jnp.concatenate([weight, weight], axis=0).T
 
-    lo_iota = lax.broadcasted_iota(I32, (128, 8 * k), 0).astype(F32)
-
     def group(g):
         w2 = w_s[pl.ds(pl.multiple_of(g * 8, 8), 8), :]
         w_flat = jnp.concatenate(
             [jnp.sum(jnp.where(m, w2, 0.0), axis=0, keepdims=True) for m in masks], axis=1)
-        right = jnp.where(lo_iota == flat[g][0:1, :], w_flat, 0.0).astype(BF16)
-        return lax.dot_general(a_s[g], right, (((1,), (1,)), ((), ())), preferred_element_type=F32)
+        w_16 = jnp.broadcast_to(w_flat, (16, 8 * k)).astype(BF16)
+        left = (a_s[g].reshape(pads // 2, 16, 8 * k) * w_16[None]).reshape(8 * pads, 8 * k)
+        return lax.dot_general(left, r_s[g], (((1,), (1,)), ((), ())), preferred_element_type=F32)
 
     def place(g, carry):
         one, two = group(g * 2), group(g * 2 + 1)
         qs = pl.ds(pl.multiple_of(g * 16, 16), 16)
         for h in range(ext):
             both = jnp.concatenate([one[h * 8:(h + 1) * 8], two[h * 8:(h + 1) * 8]], axis=0)
-            spread[qs, h * 128:(h + 1) * 128] = both.astype(BF16)
+            spread[qs, h * 256:(h + 1) * 256] = both.astype(BF16)
         return carry
 
     lax.fori_loop(0, nq // 16, place, 0, unroll=4)
@@ -298,6 +300,17 @@
     second = partial(1)
     sent_0 = pass_on(0, first)
     sent_1 = pass_on(1, second)
+
+    ones = jnp.ones((places, 128), BF16)
+    row_iota = lax.broadcasted_iota(I32, (tile, places), 0)
+    for t in range(rows // tile):
+        rs = slice(t * tile, (t + 1) * tile)
+        spots = jnp.where(row_iota + t * tile == place_i, 1.0, 0.0).astype(BF16)
+        put = jnp.dot(spots, fresh_ref[...].reshape(places, d), preferred_element_type=F32).astype(BF16)
+        keep = (1.0 - jnp.dot(spots, ones, preferred_element_type=F32)).astype(BF16)
+        for c in range(d // 128):
+            cs = slice(c * 128, (c + 1) * 128)
+            old[rs, cs] = old[rs, cs] * keep + put[:, cs]
     for c, copies in enumerate((sent_0, sent_1)):
         acc = own[c]
         for j, copy in enumerate(copies):
@@ -316,7 +329,7 @@
     k, nq = cand_t.shape
     per = nq // shards
     places = loaders * 2 * shards
-    ext = (rows + places) // 128
+    ext = (rows + places) // 256
     block, chunk = 512, 768
     anywhere = pl.BlockSpec(memory_space=pl.ANY)
     vmem = pl.BlockSpec(memory_space=pltpu.VMEM)
@@ -325,13 +338,12 @@
     return pl.pallas_call(
         functools.partial(main_kernel, block, chunk, loaders, shards),
         out_shape=[
-            jax.ShapeDtypeStruct((1, per), F32),
-            jax.ShapeDtypeStruct((per, d), F32),
-            jax.ShapeDtypeStruct((loaders, 2 * shards, d), BF16),
-            jax.ShapeDtypeStruct((8, places), F32),
+            pltpu.VMEM((1, per), F32),
+            pltpu.VMEM((per, d), F32),
+            pltpu.VMEM((rows, d), BF16),
         ],
         in_specs=[anywhere] * 3 + [vmem, smem, anywhere, vmem, vmem, vmem],
-        out_specs=[vmem] * 4,
+        out_specs=[vmem] * 3,
         scratch_shapes=[
             pltpu.VMEM((tokens, d), BF16),
             pltpu.VMEM((d, ff), BF16),
@@ -339,15 +351,15 @@
             pltpu.VMEM((2, block, ff), BF16),
             pltpu.VMEM((2, block, d), F32),
             pltpu.VMEM((tokens // LEN, d), F32),
-            pltpu.VMEM((rows, d), BF16),
+            pltpu.VMEM((loaders, 2 * shards, d), BF16),
             pltpu.VMEM((nq, rows), F32),
-            pltpu.VMEM((nq // 8, 8 * ext, 8 * k), BF16),
+            pltpu.VMEM((nq // 8, 8 * (ext + ext % 2), 8 * k), BF16),
             pltpu.VMEM((nq, 2 * k), I32),
             pltpu.VMEM((nq, 2 * k), I32),
             pltpu.VMEM((rows // 128, 128), F32),
             pltpu.VMEM((nq, 2 * k), F32),
-            pltpu.VMEM((nq // 8, 8, 8 * k), F32),
-            pltpu.VMEM((nq, 128 * ext), BF16),
+            pltpu.VMEM((nq // 8, 256, 8 * k), BF16),
+            pltpu.VMEM((nq, 256 * ext), BF16),
             pltpu.VMEM((nq, 2 * k), F32),
             pltpu.VMEM((8, 128), I32),
             pltpu.VMEM((shards, 8, 128), I32),
@@ -366,66 +378,32 @@
             dma((shards,)), dma((shards,)), dma((loaders,)), dma((loaders,)),
             dma((shards,)), dma((shards,)), dma((2, shards)), dma((2, shards)), dma((2,)), dma((2,)),
         ],
-        compiler_params=pltpu.CompilerParams(collective_id=0, has_side_effects=True, vmem_limit_bytes=60 * MIB),
+        compiler_params=pltpu.CompilerParams(collective_id=0, has_side_effects=True, vmem_limit_bytes=52 * MIB),
         name="main",
     )(hidden, w_in, w_out, gain, passage_rows, old_index, queries, cand_t, teacher_t)
 
 
-def index_kernel(tile, fresh_hbm, place_hbm, loss_hbm, grad_hbm, old_hbm, new_hbm, loss_out, grad_out,
-                 fresh_ref, place_ref, old, new, side_sem, in_sem, out_sem):
-    rows, d = old.shape
-    tiles = rows // tile
-    sides = [pltpu.make_async_copy(src, dst, side_sem.at[i]) for i, (src, dst) in enumerate(
-        [(place_hbm, place_ref), (fresh_hbm, fresh_ref), (loss_hbm, loss_out), (grad_hbm, grad_out)])]
-    loads = [pltpu.make_async_copy(old_hbm.at[pl.ds(t * tile, tile)], old.at[pl.ds(t * tile, tile)], in_sem.at[t])
-             for t in range(tiles)]
-    for load in sides[0:2] + loads + sides[2:4]:
-        load.start()
-    sides[0].wait()
-    sides[1].wait()
-    where_to = place_ref[0:1, :].astype(I32)
-    places = fresh_ref.shape[0]
-    ones = jnp.ones((places, 128), BF16)
-    row_iota = lax.broadcasted_iota(I32, (tile, places), 0)
-    stores = []
-    for t in range(tiles):
-        rs = slice(t * tile, (t + 1) * tile)
-        place = jnp.where(row_iota + t * tile == where_to, 1.0, 0.0).astype(BF16)
-        put = jnp.dot(place, fresh_ref[...], preferred_element_type=F32)
-        has = jnp.dot(place, ones, preferred_element_type=F32)
-        loads[t].wait()
-        for c in range(d // 128):
-            cs = slice(c * 128, (c + 1) * 128)
-            new[rs, cs] = jnp.where(has > 0.5, put[:, cs], old[rs, cs].astype(F32)).astype(BF16)
-        store = pltpu.make_async_copy(new.at[pl.ds(t * tile, tile)], new_hbm.at[pl.ds(t * tile, tile)], out_sem.at[t])
-        store.start()
-        stores.append(store)
-    for store in stores + sides[2:4]:
-        store.wait()
-
-
-def refresh(fresh, places, loss, grad, old_index):
-    rows, d = old_index.shape
-    tile = 512
+def results_kernel(new_in, loss_in, grad_in, new_out, loss_out, grad_out, sem):
+    copies = [pltpu.make_async_copy(src, dst, sem.at[i]) for i, (src, dst) in enumerate(
+        [(new_in, new_out), (loss_in, loss_out), (grad_in, grad_out)])]
+    for copy in copies:
+        copy.start()
+    for copy in copies:
+        copy.wait()
+
+
+def results(new, loss, grad):
     anywhere = pl.BlockSpec(memory_space=pl.ANY)
+    new, loss, grad = [pltpu.with_memory_space_constraint(v, pltpu.VMEM) for v in (new, loss, grad)]
     return pl.pallas_call(
-        functools.partial(index_kernel, tile),
-        out_shape=[jax.ShapeDtypeStruct((rows, d), BF16), jax.ShapeDtypeStruct(loss.shape, F32),
-                   jax.ShapeDtypeStruct(grad.shape, F32)],
-        in_specs=[anywhere] * 5,
+        results_kernel,
+        out_shape=[jax.ShapeDtypeStruct(v.shape, v.dtype) for v in (new, loss, grad)],
+        in_specs=[pl.BlockSpec(memory_space=pltpu.VMEM)] * 3,
         out_specs=[anywhere] * 3,
-        scratch_shapes=[
-            pltpu.VMEM(fresh.shape, BF16),
-            pltpu.VMEM(places.shape, F32),
-            pltpu.VMEM((rows, d), BF16),
-            pltpu.VMEM((rows, d), BF16),
-            pltpu.SemaphoreType.DMA((4,)),
-            pltpu.SemaphoreType.DMA((rows // tile,)),
-            pltpu.SemaphoreType.DMA((rows // tile,)),
-        ],
-        compiler_params=pltpu.CompilerParams(vmem_limit_bytes=60 * MIB),
-        name="refresh",
-    )(fresh, places, loss, grad, old_index)
+        scratch_shapes=[pltpu.SemaphoreType.DMA((3,))],
+        compiler_params=pltpu.CompilerParams(vmem_limit_bytes=16 * MIB),
+        name="results",
+    )(new, loss, grad)
 
 
 def solution(mesh):
@@ -433,9 +411,9 @@
 
     def local(hidden_states, w_in, w_out, ln_gain, passage_rows, old_index, queries, candidates, teacher):
         cand_t, teacher_t = candidates.T, teacher.T
-        loss, grad, fresh, places = main(
+        loss, grad, new = main(
             loaders, shards, hidden_states, w_in, w_out, ln_gain, passage_rows, old_index, queries, cand_t, teacher_t)
-        new_index, loss, grad = refresh(fresh.reshape(-1, fresh.shape[-1]), places, loss, grad, old_index)
+        new_index, loss, grad = results(new, loss, grad)
         return new_index, loss.reshape(-1), grad
 
     return jax.shard_map(

time: 69.9 us -> 62.7 us (0.90)
  Pallas kernels: 69 us -> 61.8 us
    pallas_call x1, Pallas kernels: 9.34 us -> 2.74 us  [results(): pl.pallas_call(results_kernel, out_shape=[jax.ShapeDtypeStruct(v.shape, v...]
where the time goes in v4:
time: 62.7 us; the launch traced here: 62.6 us
  Pallas kernels  61.8 us (99%)
  between operations  0.82 us (1%)
    pallas_call x1, Pallas kernels, main(): pl.pallas_call(functools.partial(main_kernel, block, chunk, loaders, shar...  59.1 us
    pallas_call x1, Pallas kernels, results(): pl.pallas_call(results_kernel, out_shape=[jax.ShapeDtypeStruct(v.shape, v...  2.74 us

profile of v4, /device:TPU:1, one launch (start us, length us, event | category | flops | bytes accessed | tf_op | source)
XLA Modules:
  0.0 62.6 jit_solution(12086827860730945273)
XLA Ops:
  0.6 59.1 %main.1 = (f32[1,32]{1,0:T(1,128)S(1)}, f32[32,768]{1,0:T(8,128)S(1)}, bf16[4096,768]{1,0:T(8,128)(2,1)S(1)}) custom-call(bf16[2048,768]{1,0:T(8,128)(2,1)} %x_hbm.1, bf16[768,3072]{1,0:T(8,128)(2,1)} %win_hbm.1, bf16[3072,768]{1,0:T(8,128)(2,1)} %wout_hbm.1, f32[768]{0:T(1024)} %gain_ref.1, s32[8]{0:T(128)} %rows_ref.1, bf16[4096,768]{1,0:T(8,128)(2,1)} %old_hbm.1, ...), custom_call_target="tpu_custom_call" | custom-call | tf_op jit(solution)/shard_map/main/pallas_call | solution.py:338
  59.7 2.7 %results.1 = (bf16[4096,768]{1,0:T(8,128)(2,1)}, f32[1,32]{1,0:T(1,128)}, f32[32,768]{1,0:T(8,128)}) custom-call(bf16[4096,768]{1,0:T(8,128)(2,1)S(1)} %get-tuple-element.9.new_in, f32[1,32]{1,0:T(1,128)S(1)} %get-tuple-element.10.loss_in, f32[32,768]{1,0:T(8,128)S(1)} %get-tuple-element.11.grad_in), custom_call_target="tpu_custom_call" | custom-call | tf_op jit(solution)/shard_map/results/pallas_call | solution.py:398
